TPU v7x, 512 devices: a whole 4x8x8 slice. The times are simulated.
512 devices in a mesh: rad: 32 (over z_hi, x, core), lat: 16 (over z_lo, y).
Axes of the slice: x: 4, y: 8, z: 8 (z_hi: 4, z_lo: 2; z = z_hi * 2 + z_lo), core: 2. Of those that a mesh axis runs over, the one named last changes fastest.
Arguments:
- nonlinear_samples: bfloat16 [32, 2, 1536, 3072], P('rad', None, 'lat'), may hold values from -6 to 6
- legendre: bfloat16 [256, 1536, 1024], P('rad', 'lat'), may hold values from -0.21875 to 0.21875
- assign: int32 [256], replicated, may hold values from 0 to 255, each once
- counts: int32 [256], replicated, may hold values from 513 to 1024, as said below
- spectral_state: float32 [1024, 256, 128], P('lat', 'rad'), may hold values from -6 to 6
- inverses: float32 [1024, 4, 8, 8], P('lat'), may hold values from -1 to 1
Outputs:
- advanced: float32 [1024, 256, 128], P('lat', 'rad')
Inputs may be any that keep to these rules, and one draw needn't show every extreme that they name: Slot s carries order assign[s]; each order 0 to 255 stands in exactly one slot. counts[m] is at most 1024 - m, and order 0 has 1024 live degrees.
All inputs are finite; a program needn't handle non-finite values.
Results may differ from a plain program's by a relative error of at most 0.0034.
Values may be sent and summed in bfloat16 or wider, within the bound.
A program may use at most 64 MiB of HBM per device.

v0:
```python
import math

import jax
import jax.numpy as jnp
from jax import lax
from jax.sharding import PartitionSpec as P


def trig_table(assign, lon_count):
    longitude = jnp.arange(lon_count, dtype=jnp.int32)
    phases = longitude[:, None] * assign[None, :] % lon_count
    angles = phases.astype(jnp.float32) * (2.0 * math.pi / lon_count)
    normalizing_multiplier = 1.0 / math.sqrt(lon_count)
    cosine = (jnp.cos(angles) * normalizing_multiplier).astype(jnp.bfloat16)
    sine = (-jnp.sin(angles) * normalizing_multiplier).astype(jnp.bfloat16)
    return jnp.stack([cosine, sine], axis=2).reshape(lon_count, 2 * assign.shape[0])


def radial_step(spectral_state, source, inverses, degree):
    deg_rows, slot_count, width = spectral_state.shape
    shell_number = width // 4
    blk_size = inverses.shape[2]
    blk_count = shell_number // blk_size
    field_now = spectral_state.reshape(deg_rows, slot_count, 4, shell_number)
    zero_rim = jnp.zeros((deg_rows, slot_count, 4, 1), jnp.float32)
    outward = jnp.concatenate([field_now[..., 1:], zero_rim], axis=3)
    inward = jnp.concatenate([zero_rim, field_now[..., :-1]], axis=3)
    radial_spacing = 0.65 / (shell_number + 1)
    radius = 0.35 + 0.65 * (jnp.arange(shell_number, dtype=jnp.float32) + 1.0) / (shell_number + 1)
    ratios = radial_spacing / radius
    degree_term = degree[:, None, None, None] * (degree[:, None, None, None] + 1.0)
    central = 0.5 * radial_spacing * radial_spacing * degree_term / (radius * radius)
    right_side = (
        field_now + 0.5 * (outward - 2.0 * field_now + inward) + 0.5 * ratios * (outward - inward)
    )
    right_side = (
        right_side - central * field_now + source.reshape(deg_rows, slot_count, 4, shell_number)
    )
    lower_link = -0.5 * (1.0 - ratios[0::blk_size])
    upper_link = -0.5 * (1.0 + ratios[blk_size - 1 :: blk_size])
    blocks = jnp.moveaxis(right_side.reshape(deg_rows, slot_count, 4, blk_count, blk_size), 3, 0)
    block_inverse = jnp.moveaxis(inverses, 1, 0)
    first_unit = (jnp.arange(blk_size, dtype=jnp.int32) == 0).astype(jnp.float32)
    start_carry = jnp.zeros((deg_rows, slot_count, 4), jnp.float32)

    def forward(carried, items):
        matrix, block, link = items
        block = block - link * carried[..., None] * first_unit
        result = jnp.einsum("lij,locj->loci", matrix, block, precision=lax.Precision.HIGHEST)
        return (result[..., blk_size - 1], result)

    def inverse_sweep(carried, items):
        matrix, partial_solution, link = items
        result = (
            partial_solution - link * carried[..., None] * matrix[:, None, None, :, blk_size - 1]
        )
        return (result[..., 0], result)

    _, forward_blocks = lax.scan(forward, start_carry, (block_inverse, blocks, lower_link))
    _, solved = lax.scan(
        inverse_sweep, start_carry, (block_inverse, forward_blocks, upper_link), reverse=True
    )
    return jnp.moveaxis(solved, 0, 3).reshape(deg_rows, slot_count, 4 * shell_number)


def body(nonlinear_samples, legendre, assign, counts, spectral_state, inverses):
    rad_local = nonlinear_samples.shape[0]
    lat_local = nonlinear_samples.shape[2]
    lon_count = nonlinear_samples.shape[3]
    order_total = assign.shape[0]
    order_local = legendre.shape[0]
    degree_local = spectral_state.shape[0]
    shell_grand_number = spectral_state.shape[2] // 4
    table = trig_table(assign, lon_count)
    flat_rows = nonlinear_samples.reshape(rad_local * 2 * lat_local, lon_count)
    fourier_modes = jnp.dot(flat_rows, table, preferred_element_type=jnp.float32).astype(
        jnp.bfloat16
    )
    fourier_modes = fourier_modes.reshape(rad_local, 2, lat_local, order_total, 2)
    thermal_part = lax.all_to_all(
        fourier_modes[:, 0], "rad", split_axis=2, concat_axis=0, tiled=True
    )
    magnetic_potential_part = lax.all_to_all(
        fourier_modes[:, 1], "rad", split_axis=2, concat_axis=0, tiled=True
    )
    permuted_dims = jnp.stack([thermal_part, magnetic_potential_part], axis=1)
    columns = lax.all_to_all(legendre, "lat", split_axis=2, concat_axis=1, tiled=True)
    whole = lax.all_gather(permuted_dims, "lat", axis=2, tiled=True)
    band_total = lax.axis_size("lat")
    legendre_table_bands = columns.reshape(order_local, band_total, lat_local, degree_local)
    value_bands = whole.reshape(shell_grand_number, 2, band_total, lat_local, order_local, 2)
    partial_value = jnp.einsum(
        "obtl,rfbtok->blofkr", legendre_table_bands, value_bands, preferred_element_type=jnp.float32
    )
    partial_value = lax.optimization_barrier(partial_value.astype(jnp.bfloat16)).astype(jnp.float32)
    summed = jnp.sum(partial_value, axis=0).reshape(
        degree_local, order_local, 4 * shell_grand_number
    )
    rad_position = lax.axis_index("rad")
    lat_position = lax.axis_index("lat")
    my_orders = lax.dynamic_slice_in_dim(assign, rad_position * order_local, order_local, 0)
    order_ids = jnp.arange(order_total, dtype=jnp.int32)
    my_counts = jnp.sum(
        jnp.where(my_orders[:, None] == order_ids[None, :], counts[None, :], 0), axis=1
    )
    degree_ids = lat_position * degree_local + jnp.arange(degree_local, dtype=jnp.int32)
    limits = my_orders + my_counts
    live = (degree_ids[:, None] >= my_orders[None, :]) & (degree_ids[:, None] < limits[None, :])
    source = jnp.where(live[:, :, None], summed, jnp.zeros_like(summed))
    return radial_step(spectral_state, source, inverses, degree_ids.astype(jnp.float32))


def solution(mesh):
    return jax.shard_map(
        body,
        mesh=mesh,
        in_specs=(
            P("rad", None, "lat", None),
            P("rad", "lat", None),
            P(),
            P(),
            P("lat", "rad", None),
            P("lat", None, None, None),
        ),
        out_specs=P("lat", "rad", None),
        check_vma=False,
    )
```

profile of v0, /device:TPU:6, one launch (start us, length us, event | category | flops | bytes accessed | tf_op | source)
XLA Modules:
  0.0 377.5 jit_solution(9484199052676013640)
XLA Ops:
  6.5 14.2 %multiply_convert_fusion.1 = (bf16[3072,256,1]{1,0,2:T(8,128)(2,1)S(1)}, bf16[3072,256,1]{1,0,2:T(8,128)(2,1)S(1)}) fusion(s32[256]{0:T(256)} %param.12), kind=kLoop, calls=%fused_computation.29 | loop fusion | flops 11010048 | bytes 3146752 | tf_op jit(solution)/shard_map/convert_element_type | solution.py:14
  20.7 1.9 pad_maximum_fusion
  22.7 8.8 %copy.108 = bf16[3072,256,2]{0,2,1:T(2,128)(2,1)} copy(bf16[3072,256,2]{1,0,2:T(8,128)(2,1)} %pad_maximum_fusion) | data formatting | bytes 6291456 | tf_op jit(solution)/shard_map/stack | solution.py:16
  31.4 7.5 %reshape.244 = bf16[3072,512]{0,1:T(8,128)(2,1)} reshape(bf16[3072,256,2]{0,2,1:T(2,128)(2,1)} %copy.108) | data formatting | bytes 6291456 | tf_op jit(solution)/shard_map/reshape | solution.py:16
  38.9 3.1 fusion.20
  43.6 13.4 %all-to-all-start.1 = ((bf16[1,96,256,2]{1,3,0,2:T(2,128)(2,1)}), bf16[1,96,256,2]{1,3,0,2:T(2,128)(2,1)S(1)}, u32[]{:S(2)}, u32[]{:S(2)}) async-start(bf16[1,96,256,2]{1,3,0,2:T(2,128)(2,1)} %copy.114), calls=%async_computation.1 | async-start | bytes 262144 | tf_op jit(solution)/shard_map/all_to_all | solution.py:83
  57.9 8.4 %all-to-all-done.1 = bf16[1,96,256,2]{1,3,0,2:T(2,128)(2,1)S(1)} async-done(((bf16[1,96,256,2]{1,3,0,2:T(2,128)(2,1)}), bf16[1,96,256,2]{1,3,0,2:T(2,128)(2,1)S(1)}, u32[]{:S(2)}, u32[]{:S(2)}) %all-to-all-start.1) | async-done | bytes 98336 | tf_op jit(solution)/shard_map/all_to_all | solution.py:83
  66.4 5.8 %all-to-all-start = ((bf16[1,96,256,2]{1,3,0,2:T(2,128)(2,1)}), bf16[1,96,256,2]{1,3,0,2:T(2,128)(2,1)S(1)}, u32[]{:S(2)}, u32[]{:S(2)}) async-start(bf16[1,96,256,2]{1,3,0,2:T(2,128)(2,1)} %copy.111), calls=%async_computation | async-start | bytes 262144 | tf_op jit(solution)/shard_map/all_to_all | solution.py:80
  72.2 9.2 %all-to-all-done = bf16[1,96,256,2]{1,3,0,2:T(2,128)(2,1)S(1)} async-done(((bf16[1,96,256,2]{1,3,0,2:T(2,128)(2,1)}), bf16[1,96,256,2]{1,3,0,2:T(2,128)(2,1)S(1)}, u32[]{:S(2)}, u32[]{:S(2)}) %all-to-all-start) | async-done | bytes 98336 | tf_op jit(solution)/shard_map/all_to_all | solution.py:80
  81.4 2.2 copy.116
  83.7 2.9 copy.118
  86.6 7.8 %all-to-all-start.2 = ((bf16[8,96,1024]{1,0,2:T(8,128)(2,1)}), bf16[8,96,1024]{1,0,2:T(8,128)(2,1)}, u32[]{:S(2)}, u32[]{:S(2)}) async-start(bf16[8,96,1024]{1,0,2:T(8,128)(2,1)} %copy.118), calls=%async_computation.2 | async-start | bytes 4194304 | tf_op jit(solution)/shard_map/all_to_all | solution.py:87
  94.9 1.3 copy.122
  96.8 71.1 %all-to-all-done.2 = bf16[8,96,1024]{1,0,2:T(8,128)(2,1)} async-done(((bf16[8,96,1024]{1,0,2:T(8,128)(2,1)}), bf16[8,96,1024]{1,0,2:T(8,128)(2,1)}, u32[]{:S(2)}, u32[]{:S(2)}) %all-to-all-start.2) | async-done | bytes 1572896 | tf_op jit(solution)/shard_map/all_to_all | solution.py:87
  167.9 103.0 %all-gather.2.cloned.1.call-done = bf16[32,2,1536,8,2]{0,3,4,1,2:T(8,128)(2,1)} async-done(((bf16[32,2,96,8,2]{0,3,4,1,2:T(8,128)(2,1)}), bf16[32,2,1536,8,2]{0,3,4,1,2:T(8,128)(2,1)}) %all-gather.2.cloned.1.call-update) | async-done | bytes 3145744 | tf_op jit(solution)/shard_map/all_gather | solution.py:88
  270.9 8.7 %convert_bitcast_fusion = bf16[16,64,8,2,2,32]{1,5,4,3,2,0:T(8,128)(2,1)S(1)} fusion(bf16[32,2,16,96,8,2]{0,4,5,1,3,2:T(8,128)(2,1)} %bitcast.114, bf16[8,96,16,64]{1,0,3,2:T(8,128)(2,1)} %bitcast.15), kind=kOutput, calls=%fused_computation.24 | convolution fusion | flops 202375168 | bytes 6815744 | tf_op jit(solution)/shard_map/obtl,rfbtok->blofkr/dot_general | solution.py:92
  279.6 1.0 convert_reduce_fusion
  280.5 1.1 add_bitcast_fusion
  282.5 77.8 %while.30 = (s32[]{:T(128)}, f32[64,8,4]{1,2,0:T(4,128)S(1)}, f32[4,64,8,4,8]{1,4,3,2,0:T(8,128)}, f32[4,64,8,4,8]{1,4,0,3,2:T(8,128)}, f32[4]{0:T(128)S(1)}, /*index=5*/f32[4,64,8,8]{3,2,1,0:T(8,128)}, s32[]{:T(128)}) while((s32[]{:T(128)}, f32[64,8,4]{1,2,0:T(4,128)S(1)}, f32[4,64,8,4,8]{1,4,3,2,0:T(8,128)}, ...), condition=%wide.region_3.4_spmd.clone, body=%wide.region_2.3_spmd.clone.sunk | while | flops 1607698 | bytes 1025185 | solution.py:59
  285.6 14.9 %fusion.30 = f32[64,8,4,8]{1,3,2,0:T(8,128)S(1)} fusion(f32[1,64,8,4,8]{4,2,3,1,0:T(8,128)S(1)} %copy.162, f32[8]{0:T(128)S(1)} %compare_convert_fusion.2, f32[64,8,4]{1,2,0:T(4,128)S(1)} %bitcast.101, f32[4,64,8,8]{3,2,1,0:T(8,128)} %get-tuple-element.387, s32[]{:T(128)} %get-tuple-element.375), kind=kOutput, calls=%fused_computation.9.clone.1 | convolution fusion | flops 1605632 | bytes 401952 | tf_op jit(solution)/shard_map/while/body/eval_jaxpr/lij,locj->loci/dot_general | solution.py:49
  305.1 14.9 %fusion.30 = f32[64,8,4,8]{1,3,2,0:T(8,128)S(1)} fusion(f32[1,64,8,4,8]{4,2,3,1,0:T(8,128)S(1)} %copy.162, f32[8]{0:T(128)S(1)} %compare_convert_fusion.2, f32[64,8,4]{1,2,0:T(4,128)S(1)} %bitcast.101, f32[4,64,8,8]{3,2,1,0:T(8,128)} %get-tuple-element.387, s32[]{:T(128)} %get-tuple-element.375), kind=kOutput, calls=%fused_computation.9.clone.1 | convolution fusion | flops 1605632 | bytes 401952 | tf_op jit(solution)/shard_map/while/body/eval_jaxpr/lij,locj->loci/dot_general | solution.py:49
  324.5 14.9 %fusion.30 = f32[64,8,4,8]{1,3,2,0:T(8,128)S(1)} fusion(f32[1,64,8,4,8]{4,2,3,1,0:T(8,128)S(1)} %copy.162, f32[8]{0:T(128)S(1)} %compare_convert_fusion.2, f32[64,8,4]{1,2,0:T(4,128)S(1)} %bitcast.101, f32[4,64,8,8]{3,2,1,0:T(8,128)} %get-tuple-element.387, s32[]{:T(128)} %get-tuple-element.375), kind=kOutput, calls=%fused_computation.9.clone.1 | convolution fusion | flops 1605632 | bytes 401952 | tf_op jit(solution)/shard_map/while/body/eval_jaxpr/lij,locj->loci/dot_general | solution.py:49
  344.0 14.9 %fusion.30 = f32[64,8,4,8]{1,3,2,0:T(8,128)S(1)} fusion(f32[1,64,8,4,8]{4,2,3,1,0:T(8,128)S(1)} %copy.162, f32[8]{0:T(128)S(1)} %compare_convert_fusion.2, f32[64,8,4]{1,2,0:T(4,128)S(1)} %bitcast.101, f32[4,64,8,8]{3,2,1,0:T(8,128)} %get-tuple-element.387, s32[]{:T(128)} %get-tuple-element.375), kind=kOutput, calls=%fused_computation.9.clone.1 | convolution fusion | flops 1605632 | bytes 401952 | tf_op jit(solution)/shard_map/while/body/eval_jaxpr/lij,locj->loci/dot_general | solution.py:49
  360.4 9.2 %while.29 = (s32[]{:T(128)}, f32[64,8,4]{0,2,1:T(4,128)S(1)}, f32[4,64,8,4,8]{1,4,3,2,0:T(8,128)S(1)}, f32[4,64,8,4,8]{1,4,3,2,0:T(8,128)}, f32[4]{0:T(128)S(1)}...) while((s32[]{:T(128)}, f32[64,8,4]{0,2,1:T(4,128)S(1)}, f32[4,64,8,4,8]{1,4,3,2,0:T(8,128)S(1)}, ...), condition=%wide.region_5.6_spmd, body=%wide.region_4.5_spmd.sunk | while | flops 38915 | bytes 459641 | solution.py:60
  (110 shorter events, 32.5 us)
Async XLA Ops:
  6.5 32.4 %copy-start = (bf16[1,2,96,3072]{3,2,1,0:T(8,128)(2,1)S(1)}, bf16[1,2,96,3072]{3,2,1,0:T(8,128)(2,1)}, u32[]{:S(2)}) copy-start(bf16[1,2,96,3072]{3,2,1,0:T(8,128)(2,1)} %param.10) | copy-start | bytes 3538948
  42.2 41.5 %copy-start.1 = (bf16[8,96,1024]{2,1,0:T(8,128)(2,1)S(1)}, bf16[8,96,1024]{2,1,0:T(8,128)(2,1)}, u32[]{:S(2)}) copy-start(bf16[8,96,1024]{2,1,0:T(8,128)(2,1)} %param.11) | copy-start | bytes 4718596
  43.6 22.7 %all-to-all-start.1 = ((bf16[1,96,256,2]{1,3,0,2:T(2,128)(2,1)}), bf16[1,96,256,2]{1,3,0,2:T(2,128)(2,1)S(1)}, u32[]{:S(2)}, u32[]{:S(2)}) async-start(bf16[1,96,256,2]{1,3,0,2:T(2,128)(2,1)} %copy.114), calls=%async_computation.1 | async-start | bytes 262144 | tf_op jit(solution)/shard_map/all_to_all | solution.py:83
  66.4 15.0 %all-to-all-start = ((bf16[1,96,256,2]{1,3,0,2:T(2,128)(2,1)}), bf16[1,96,256,2]{1,3,0,2:T(2,128)(2,1)S(1)}, u32[]{:S(2)}, u32[]{:S(2)}) async-start(bf16[1,96,256,2]{1,3,0,2:T(2,128)(2,1)} %copy.111), calls=%async_computation | async-start | bytes 262144 | tf_op jit(solution)/shard_map/all_to_all | solution.py:80
  72.1 198.8 %all-gather.2.cloned.1.call-start = ((), (), s32[]{:S(2)}) async-start(), calls=%async_computation.3 | async-start | bytes 13369344 | tf_op jit(solution)/shard_map/all_gather | solution.py:88
  83.6 10.9 %copy-start.4 = (s32[256]{0:T(256)S(1)}, s32[256]{0:T(256)}, u32[]{:S(2)}) copy-start(s32[256]{0:T(256)} %param.12) | copy-start | bytes 3076
  83.7 11.0 %copy-start.3 = (f32[64,8,128]{2,1,0:T(8,128)S(1)}, f32[64,8,128]{2,1,0:T(8,128)}, u32[]{:S(2)}) copy-start(f32[64,8,128]{2,1,0:T(8,128)} %param.14) | copy-start | bytes 786436
  86.5 8.3 %copy-start.2 = (f32[64,4,8,8]{0,3,2,1:T(8,128)S(1)}, f32[64,4,8,8]{0,3,2,1:T(8,128)}, u32[]{:S(2)}) copy-start(f32[64,4,8,8]{0,3,2,1:T(8,128)} %param.15) | copy-start | bytes 196612
  86.6 9.7 %copy-start.5 = (s32[256]{0:T(256)S(1)}, s32[256]{0:T(256)}, u32[]{:S(2)}) copy-start(s32[256]{0:T(256)} %param.13) | copy-start | bytes 3076
  86.6 81.3 %all-to-all-start.2 = ((bf16[8,96,1024]{1,0,2:T(8,128)(2,1)}), bf16[8,96,1024]{1,0,2:T(8,128)(2,1)}, u32[]{:S(2)}, u32[]{:S(2)}) async-start(bf16[8,96,1024]{1,0,2:T(8,128)(2,1)} %copy.118), calls=%async_computation.2 | async-start | bytes 4194304 | tf_op jit(solution)/shard_map/all_to_all | solution.py:87
Sparse Core Ops, SparseCore 0:
  83.8 187.0 all-gather.1
where the time goes:
time: 379 us; the launch traced here: 377 us
  waiting for transfers between devices  192 us (51%)
  matrix products  71.3 us (19%)
  local copies, waits for them, and re-layouts  45.8 us (12%)
  other arithmetic  27.6 us (7%)
  starting transfers between devices  27 us (7%)
  between operations  13.6 us (4%)
    all_gather x1, waiting for transfers between devices, body(): whole = lax.all_gather(permuted_dims, 'lat', axis=2, tiled=True)  103 us
    all_to_all x1, waiting for transfers between devices, body(): lax.all_to_all(legendre, 'lat', split_axis=2, concat_axis=1, tiled=True)  71.1 us
    dot_general x4, matrix products, forward(): jnp.einsum('lij,locj->loci', matrix, block, precision=lax.Precision.HIGHEST)  59.6 us
    convert_element_type x1, other arithmetic, trig_table(): cosine = (jnp.cos(angles) * normalizing_multiplier).astype(jnp.bfloat16)  14.2 us
    all_to_all x1, starting transfers between devices, body(): lax.all_to_all(fourier_modes[:, 1], 'rad', split_axis=2, concat_axis=0, t...  13.4 us
    dynamic_slice x24, local copies, waits for them, and re-layouts, radial_step(): lax.scan(forward, start_carry, (block_inverse, blocks, lower_link))  12.4 us
    all_to_all x1, waiting for transfers between devices, body(): lax.all_to_all(fourier_modes[:, 0], 'rad', split_axis=2, concat_axis=0, t...  9.16 us
    another operation x1, local copies, waits for them, and re-layouts, trig_table(): jnp.stack([cosine, sine], axis=2).reshape(lon_count, 2 * assign.shape[0])  8.76 us
  transfers between devices with their start and end apart: 4, of which 4 were waited for; matrix products, arithmetic and copies ran while one was open for 2% of the time, Pallas kernels for 0%

commit v1 on v0

v1 whole, which is shorter than its diff:
```python
import functools
import math

import jax
import jax.numpy as jnp
from jax import lax
from jax.experimental import pallas as pl
from jax.experimental.pallas import tpu as pltpu
from jax.sharding import PartitionSpec as P

MESH = pl.DeviceIdType.MESH
F32 = jnp.float32
BF16 = jnp.bfloat16
FAR = ((0, 1), (2, 3))


def kernel(
    n_rad,
    samples,
    legendre,
    cos_a,
    sin_a,
    cos_b,
    sin_b,
    state,
    inverses,
    live,
    out,
    table,
    send_rows,
    got_rows,
    rows32,
    modes,
    leg_own,
    leg_got,
    leg_mat,
    send_buf,
    recv_buf,
    acc,
    fields,
    right,
    solved,
    own_sem,
    zs_sem,
    zr_sem,
    as_sem,
    ar_sem,
    rs_sem,
    rr_sem,
):
    rad = lax.axis_index("rad")
    lat = lax.axis_index("lat")
    z = lat // 8
    y = lat % 8
    other = (1 - z) * 8 + y
    y_next = (z * 8 + (y + 1) % 8, z * 8 + (y + 7) % 8)
    n_r = n_rad
    kb = n_r // 4
    comps = 4 * n_r
    lon_a = cos_a.shape[0]
    lon_b = cos_b.shape[0]
    slots = cos_a.shape[1]

    barrier = pltpu.get_barrier_semaphore()

    @pl.loop(1, n_rad)
    def _(i):
        peer = (rad + i) % n_rad
        pl.semaphore_signal(barrier, inc=1, device_id=(peer, lat), device_id_type=MESH)
        pl.semaphore_signal(barrier, inc=1, device_id=(peer, other), device_id_type=MESH)

    pl.semaphore_signal(barrier, inc=1, device_id=(rad, other), device_id_type=MESH)
    for d in range(2):
        pl.semaphore_signal(barrier, inc=1, device_id=(rad, y_next[d]), device_id_type=MESH)

    tile_of = [(y // 2 + o) % 4 for o in (2, 1, 3, 0)]

    def own_copy(c):
        lanes = pl.multiple_of(z * 512 + tile_of[c] * 128, 128)
        return pltpu.make_async_copy(
            legendre.at[:, :, pl.ds(lanes, 128)], leg_own.at[tile_of[c]], own_sem.at[c]
        )

    def z_copy(c):
        lanes = pl.multiple_of((1 - z) * 512 + tile_of[c] * 128, 128)
        return pltpu.make_async_remote_copy(
            src_ref=legendre.at[:, :, pl.ds(lanes, 128)],
            dst_ref=leg_got.at[tile_of[c]],
            send_sem=zs_sem.at[c],
            recv_sem=zr_sem.at[c],
            device_id=(rad, other),
            device_id_type=MESH,
        )

    for c in range(4):
        own_copy(c).start()

    @pl.loop(0, lon_a)
    def _(a):
        ca = cos_a[pl.ds(a, 1), :]
        sa = sin_a[pl.ds(a, 1), :]
        cb = cos_b[...]
        sb = sin_b[...]
        at = pl.multiple_of(a * lon_b, lon_b)
        table[pl.ds(at, lon_b), 0:slots] = (ca * cb - sa * sb).astype(BF16)
        table[pl.ds(at, lon_b), slots : 2 * slots] = (-(sa * cb + ca * sb)).astype(BF16)

    pl.semaphore_wait(barrier, 2 * (n_rad - 1) + 3)
    for c in range(4):
        z_copy(c).start()

    fourier = jnp.dot(samples[...], table[...], preferred_element_type=F32)
    fourier = fourier.astype(BF16).astype(F32)
    for f in range(2):
        part = fourier[96 * f : 96 * (f + 1)]
        part = jnp.concatenate([part, jnp.zeros((32, 2 * slots), F32)], axis=0)
        flipped = part.T
        both = jnp.concatenate(
            [
                flipped[:slots].reshape(n_rad, 8, 128),
                flipped[slots:].reshape(n_rad, 8, 128),
            ],
            axis=1,
        )
        send_rows[:, 16 * f : 16 * (f + 1), :] = both.astype(BF16)

    def a2a(peer, other_side):
        return pltpu.make_async_remote_copy(
            src_ref=send_rows.at[peer],
            dst_ref=got_rows.at[z, rad],
            send_sem=as_sem.at[other_side],
            recv_sem=ar_sem.at[other_side],
            device_id=(peer, other if other_side else lat),
            device_id_type=MESH,
        )

    a2a(rad, 1).start()

    @pl.loop(1, n_rad)
    def _(i):
        peer = (rad + i) % n_rad
        a2a(peer, 0).start()
        a2a(peer, 1).start()

    got_rows[z, rad] = send_rows[rad]

    leg_mat[:, :, :, 96:128, :] = jnp.zeros((2, 8, 4, 32, 128), BF16)
    leg_mat[:, :, :, 224:256, :] = jnp.zeros((2, 8, 4, 32, 128), BF16)
    low = lax.broadcasted_iota(jnp.int32, (96, 128), 1) < 64

    def lay(source, band, tile):
        @pl.loop(0, 4)
        def _(p):
            a = source[tile, 2 * p].astype(F32)
            b = source[tile, 2 * p + 1].astype(F32)
            ra = pltpu.roll(a, 64, 1)
            rb = pltpu.roll(b, 64, 1)
            zero = jnp.zeros_like(a)
            leg_mat[band, 2 * tile, p, 0:96, :] = jnp.where(low, a, zero).astype(BF16)
            leg_mat[band, 2 * tile, p, 128:224, :] = jnp.where(low, zero, rb).astype(BF16)
            leg_mat[band, 2 * tile + 1, p, 0:96, :] = jnp.where(low, ra, zero).astype(BF16)
            leg_mat[band, 2 * tile + 1, p, 128:224, :] = jnp.where(low, zero, b).astype(BF16)

    for c in range(4):
        own_copy(c).wait()
        lay(leg_own, 0, tile_of[c])

    for p in range(4):
        pair = jnp.concatenate(
            [state[pl.ds(2 * p, 64, stride=8), :], state[pl.ds(2 * p + 1, 64, stride=8), :]], axis=0
        )
        fields[comps * p : comps * (p + 1), :] = pair.T

    spacing = 0.65 / (n_r + 1)
    radius = [0.35 + 0.65 * (i + 1.0) / (n_r + 1) for i in range(n_r)]
    degree = (lat * 64 + lax.broadcasted_iota(jnp.int32, (1, 128), 1) % 64).astype(F32)
    square = 0.5 * spacing * spacing * degree * (degree + 1.0)
    for i in range(n_r):
        now = fields[pl.ds(i, 16, stride=n_r), :]
        value = -(square * (1.0 / (radius[i] * radius[i]))) * now
        ratio = spacing / radius[i]
        if i + 1 < n_r:
            value = value + (0.5 + 0.5 * ratio) * fields[pl.ds(i + 1, 16, stride=n_r), :]
        if i > 0:
            value = value + (0.5 - 0.5 * ratio) * fields[pl.ds(i - 1, 16, stride=n_r), :]
        right[pl.ds(i, 16, stride=n_r), :] = value

    def regroup(band, side):
        rows32[...] = got_rows[band].reshape(n_rad * 32, 128).astype(F32)
        for s in range(8):
            for c in range(4):
                modes[side, s // 2, n_r * c : n_r * (c + 1), 128 * (s % 2) : 128 * (s % 2 + 1)] = (
                    rows32[pl.ds(8 * c + s, n_r, stride=32), :].astype(BF16)
                )

    def arrival(side, first):
        band = z if side == 0 else 1 - z
        return pltpu.make_async_remote_copy(
            src_ref=send_rows.at[pl.ds(first, n_rad - first)],
            dst_ref=got_rows.at[band, pl.ds(first, n_rad - first)],
            send_sem=as_sem.at[side],
            recv_sem=ar_sem.at[side],
            device_id=(rad, other),
            device_id_type=MESH,
        )

    arrival(0, 1).wait_recv()
    regroup(z, 0)
    arrival(1, 0).wait_recv()
    regroup(1 - z, 1)

    def own(d, p):
        total = None
        for side in range(2):
            band = jnp.dot(modes[side, p], leg_mat[side, d, p], preferred_element_type=F32)
            band = band.astype(BF16).astype(F32)
            total = band if total is None else total + band
        return total

    def hop(way, h, p):
        i = (way * 4 + h - 1) * 4 + p
        return pltpu.make_async_remote_copy(
            src_ref=send_buf.at[way, h - 1, p],
            dst_ref=recv_buf.at[way, h - 1, p],
            send_sem=rs_sem.at[i],
            recv_sem=rr_sem.at[i],
            device_id=(rad, y_next[way]),
            device_id_type=MESH,
        )

    for h in (4, 3, 2, 1):
        for c in {4: (0,), 3: (1, 2), 2: (), 1: (3,)}[h]:
            z_copy(c).wait_recv()
            lay(leg_got, 1, tile_of[c])
        for p in range(4):
            for way in range(2):
                if h == 4 and p not in FAR[way]:
                    continue
                d = (y + h) % 8 if way == 0 else (y + 8 - h) % 8
                total = own(d, p)
                if h < 3 or (h == 3 and p in FAR[way]):
                    hop(way, h + 1, p).wait_recv()
                    total = total + recv_buf[way, h, p]
                send_buf[way, h - 1, p] = total
                hop(way, h, p).start()

    for p in range(4):
        acc[comps * p : comps * (p + 1), :] = own(y, p)
    for p in range(4):
        total = acc[comps * p : comps * (p + 1), :]
        for way in range(2):
            hop(way, 1, p).wait_recv()
            total = total + recv_buf[way, 0, p]
        total = jnp.where(live[p : p + 1, :] > 0, total, jnp.zeros_like(total))
        rows = slice(comps * p, comps * (p + 1))
        right[rows, :] = right[rows, :] + total

    ratios = [spacing / radius[i] for i in range(n_r)]
    lower = [-0.5 * (1.0 - ratios[k * kb]) for k in range(4)]
    upper = [-0.5 * (1.0 + ratios[(k + 1) * kb - 1]) for k in range(4)]
    carried = None
    forward = []
    for k in range(4):
        b = [right[pl.ds(k * kb + j, 16, stride=n_r), :] for j in range(kb)]
        if k > 0:
            b[0] = b[0] - lower[k] * carried
        rows = []
        for i in range(kb):
            value = None
            for j in range(kb):
                at = (k * kb + i) * kb + j
                term = inverses[at : at + 1, :] * b[j]
                value = term if value is None else value + term
            rows.append(value)
        forward.append(rows)
        carried = rows[kb - 1]
    carried = None
    for k in (3, 2, 1, 0):
        rows = forward[k]
        if k < 3:
            scaled = upper[k] * carried
            rows = [
                rows[i]
                - scaled * inverses[(k * kb + i) * kb + kb - 1 : (k * kb + i) * kb + kb, :]
                for i in range(kb)
            ]
        carried = rows[0]
        for i in range(kb):
            solved[pl.ds(k * kb + i, 16, stride=n_r), :] = rows[i]
    for p in range(4):
        flipped = solved[comps * p : comps * (p + 1), :].T
        out[pl.ds(2 * p, 64, stride=8), :] = flipped[:64]
        out[pl.ds(2 * p + 1, 64, stride=8), :] = flipped[64:]

    for c in range(4):
        z_copy(c).wait_send()
    arrival(0, 1).wait_send()
    arrival(1, 0).wait_send()
    for h in (4, 3, 2, 1):
        for p in range(4):
            for way in range(2):
                if h < 4 or p in FAR[way]:
                    hop(way, h, p).wait_send()


def body(n_rad, samples, legendre, assign, counts, spectral_state, inverses):
    lon = samples.shape[3]
    lon_b = 32
    lon_a = lon // lon_b
    rad = lax.axis_index("rad")
    lat = lax.axis_index("lat")
    kb = inverses.shape[2]
    n_r = 4 * kb
    comps = 4 * n_r
    order = assign[None, :]
    phase_a = jnp.arange(lon_a, dtype=jnp.int32)[:, None] * order % lon_a
    phase_b = jnp.arange(lon_b, dtype=jnp.int32)[:, None] * order % lon
    angle_a = phase_a.astype(F32) * (2.0 * math.pi / lon_a)
    angle_b = phase_b.astype(F32) * (2.0 * math.pi / lon)
    unit = 1.0 / math.sqrt(lon)
    cos_a, sin_a = jnp.cos(angle_a), jnp.sin(angle_a)
    cos_b, sin_b = jnp.cos(angle_b) * unit, jnp.sin(angle_b) * unit

    mine = lax.dynamic_slice_in_dim(assign, rad * 8, 8, 0)
    ids = jnp.arange(counts.shape[0], dtype=jnp.int32)
    held = jnp.sum(jnp.where(mine[:, None] == ids[None, :], counts[None, :], 0), axis=1)
    degrees = lat * 64 + jnp.arange(64, dtype=jnp.int32)
    live = (degrees[None, :] >= mine[:, None]) & (degrees[None, :] < (mine + held)[:, None])
    live = live.astype(F32).reshape(4, 128)

    inv = jnp.transpose(inverses, (1, 2, 3, 0)).reshape(4 * kb * kb, 64)
    inv = jnp.concatenate([inv, inv], axis=1)

    vmem = pl.BlockSpec(memory_space=pltpu.VMEM)
    out = pl.pallas_call(
        functools.partial(kernel, n_rad),
        out_shape=jax.ShapeDtypeStruct((512, comps), F32),
        in_specs=[vmem, pl.BlockSpec(memory_space=pl.ANY)] + [vmem] * 7,
        out_specs=vmem,
        scratch_shapes=[
            pltpu.VMEM((lon, 2 * assign.shape[0]), BF16),
            pltpu.VMEM((n_rad, 32, 128), BF16),
            pltpu.VMEM((2, n_rad, 32, 128), BF16),
            pltpu.VMEM((n_rad * 32, 128), F32),
            pltpu.VMEM((2, 4, comps, 256), BF16),
            pltpu.VMEM((4, 8, 96, 128), BF16),
            pltpu.VMEM((4, 8, 96, 128), BF16),
            pltpu.VMEM((2, 8, 4, 256, 128), BF16),
            pltpu.VMEM((2, 4, 4, comps, 128), F32),
            pltpu.VMEM((2, 4, 4, comps, 128), F32),
            pltpu.VMEM((4 * comps, 128), F32),
            pltpu.VMEM((4 * comps, 128), F32),
            pltpu.VMEM((4 * comps, 128), F32),
            pltpu.VMEM((4 * comps, 128), F32),
            pltpu.SemaphoreType.DMA((4,)),
            pltpu.SemaphoreType.DMA((4,)),
            pltpu.SemaphoreType.DMA((4,)),
            pltpu.SemaphoreType.DMA((2,)),
            pltpu.SemaphoreType.DMA((2,)),
            pltpu.SemaphoreType.DMA((32,)),
            pltpu.SemaphoreType.DMA((32,)),
        ],
        compiler_params=pltpu.CompilerParams(
            collective_id=0, has_side_effects=True, vmem_limit_bytes=48 * 1024 * 1024
        ),
    )(
        samples.reshape(192, lon),
        legendre,
        cos_a,
        sin_a,
        cos_b,
        sin_b,
        spectral_state.reshape(512, comps),
        inv,
        live,
    )
    return out.reshape(64, 8, comps)


def solution(mesh):
    return jax.shard_map(
        functools.partial(body, mesh.shape["rad"]),
        mesh=mesh,
        in_specs=(
            P("rad", None, "lat", None),
            P("rad", "lat", None),
            P(),
            P(),
            P("lat", "rad", None),
            P("lat", None, None, None),
        ),
        out_specs=P("lat", "rad", None),
        check_vma=False,
    )
```

time: 379 us -> 82.2 us (0.22)
  waiting for transfers between devices: 192 us -> 0 us
  Pallas kernels: 0 us -> 71.6 us
  matrix products: 71.3 us -> 0 us
  local copies, waits for them, and re-layouts: 45.8 us -> 5.64 us
  starting transfers between devices: 27 us -> 0 us
  other arithmetic: 27.6 us -> 4.65 us
  between operations: 13.6 us -> 0.03 us
    all_gather x1 -> x0, waiting for transfers between devices: 103 us -> none  [body(): whole = lax.all_gather(permuted_dims, 'lat', axis=2, tiled=True)]
    all_to_all x3 -> x0, waiting for transfers between devices: 88.7 us -> none  [the longest x1 71.1 us: body(): lax.all_to_all(legendre, 'lat', split_axis=2, concat_axis=1, tiled=True)]
    pallas_call x0 -> x1, Pallas kernels: none -> 71.6 us  [body(): pl.pallas_call(functools.partial(kernel, n_rad), out_shape=jax.ShapeDtype...]
    dot_general x6 -> x0, matrix products: 71.3 us -> none  [the longest x4 59.6 us: forward(): jnp.einsum('lij,locj->loci', matrix, block, precision=lax.Precision.HIGHEST)]
    all_to_all x3 -> x0, starting transfers between devices: 26.9 us -> none  [the longest x1 13.4 us: body(): lax.all_to_all(fourier_modes[:, 1], 'rad', split_axis=2, concat_axis=0, t...]
    convert_element_type x5 -> x1, other arithmetic: 14.2 us -> 0.01 us  [body(): live = live.astype(F32).reshape(4, 128)]
    another operation x4 -> x0, local copies, waits for them, and re-layouts: 11.8 us -> none  [the longest x1 8.76 us: trig_table(): jnp.stack([cosine, sine], axis=2).reshape(lon_count, 2 * assign.shape[0])]
    dynamic_slice x25 -> x1, local copies, waits for them, and re-layouts: 12.5 us -> 0.75 us  [body(): mine = lax.dynamic_slice_in_dim(assign, rad * 8, 8, 0)]
  transfers between devices with their start and end apart: 4 -> 0, of which waited for: 4 -> 0; matrix products, arithmetic and copies ran while one was open for 2% -> 0% of each run, Pallas kernels for 0% -> 0%
where the time goes in v1:
time: 82.2 us; the launch traced here: 81.9 us
  Pallas kernels  71.6 us (87%)
  local copies, waits for them, and re-layouts  5.64 us (7%)
  other arithmetic  4.65 us (6%)
    pallas_call x1, Pallas kernels, body(): pl.pallas_call(functools.partial(kernel, n_rad), out_shape=jax.ShapeDtype...  71.6 us
    unnamed x7, local copies, waits for them, and re-layouts  4.33 us

profile of v1, /device:TPU:6, one launch (start us, length us, event | category | flops | bytes accessed | tf_op | source)
XLA Modules:
  0.0 81.9 jit_solution(12322504592873900314)
XLA Ops:
  0.0 0.8 dynamic_slice.3
  0.8 0.9 %select_reduce_fusion = s32[8]{0:T(128)S(1)} fusion(s32[256]{0:T(256)} %param.9, s32[8]{0:T(128)S(1)} %dynamic_slice.3), kind=kLoop, calls=%fused_computation.19 | loop fusion | flops 6136 | bytes 1088 | tf_op jit(solution)/shard_map/reduce_sum | solution.py:326
  1.6 0.8 dynamic-slice_add_fusion
  2.4 0.1 ge.23
  2.5 0.1 lt.34
  2.5 0.1 ge.25
  2.6 0.1 ge.26
  2.7 0.1 ge.27
  2.8 0.1 lt.35
  2.9 0.1 lt.36
  2.9 0.8 %sine_multiply_fusion = (f32[32,256]{1,0:T(8,128)S(1)}, f32[32,256]{1,0:T(8,128)S(1)}) fusion(s32[256]{0:T(256)} %param.8), kind=kLoop, calls=%fused_computation.13 | loop fusion | flops 90112 | bytes 66560 | tf_op jit(solution)/shard_map/mul | solution.py:322
  3.8 1.1 %pad_maximum_fusion.inverses = f32[256,128]{1,0:T(8,128)S(1)} fusion(f32[256,64]{1,0:T(8,128)} %bitcast.9), kind=kLoop, calls=%fused_computation.1 | loop fusion | flops 32768 | bytes 196608 | tf_op jit(solution)/shard_map/concatenate | solution.py:332
  4.9 1.1 %fusion.4 = (f32[96,256]{1,0:T(8,128)S(1)}, f32[96,256]{1,0:T(8,128)S(1)}) fusion(s32[256]{0:T(256)} %param.8), kind=kLoop, calls=%fused_computation.7 | loop fusion | flops 221184 | bytes 197632 | tf_op jit(solution)/shard_map/sin | solution.py:321
  6.0 0.0 copy-start
  6.0 1.4 %copy-done = bf16[8,96,1024]{2,1,0:T(8,128)(2,1)S(1)} copy-done((bf16[8,96,1024]{2,1,0:T(8,128)(2,1)S(1)}, bf16[8,96,1024]{2,1,0:T(8,128)(2,1)}, u32[]{:S(2)}) %copy-start) | copy-done | bytes 1572888
  7.4 0.0 copy-start.1
  7.4 1.3 %copy-done.1 = bf16[1,2,96,3072]{3,2,1,0:T(8,128)(2,1)S(1)} copy-done((bf16[1,2,96,3072]{3,2,1,0:T(8,128)(2,1)S(1)}, bf16[1,2,96,3072]{3,2,1,0:T(8,128)(2,1)}, u32[]{:S(2)}) %copy-start.1) | copy-done | bytes 1179672
  8.7 0.0 copy-start.2
  8.7 0.9 %copy-done.2 = f32[64,8,128]{2,1,0:T(8,128)S(1)} copy-done((f32[64,8,128]{2,1,0:T(8,128)S(1)}, f32[64,8,128]{2,1,0:T(8,128)}, u32[]{:S(2)}) %copy-start.2) | copy-done | bytes 262168
  9.6 71.6 %shard_map.64 = f32[512,128]{1,0:T(8,128)S(1)} custom-call(bf16[192,3072]{1,0:T(8,128)(2,1)S(1)} %bitcast.6, bf16[8,96,1024]{2,1,0:T(8,128)(2,1)S(1)} %copy-done, f32[96,256]{1,0:T(8,128)S(1)} %get-tuple-element.8.cos_a, f32[96,256]{1,0:T(8,128)S(1)} %get-tuple-element.7.sin_a, f32[32,256]{1,0:T(8,128)S(1)} %get-tuple-element.6.cos_b, ...), custom_call_target="tpu_custom_call" | custom-call | tf_op jit(solution)/shard_map/pallas_call | solution.py:335
  81.2 0.7 copy.8
  (3 shorter events, 0.0 us)
Async XLA Ops:
  6.0 1.4 %copy-start = (bf16[8,96,1024]{2,1,0:T(8,128)(2,1)S(1)}, bf16[8,96,1024]{2,1,0:T(8,128)(2,1)}, u32[]{:S(2)}) copy-start(bf16[8,96,1024]{2,1,0:T(8,128)(2,1)} %legendre.1) | copy-start | bytes 4718596
  7.4 1.3 %copy-start.1 = (bf16[1,2,96,3072]{3,2,1,0:T(8,128)(2,1)S(1)}, bf16[1,2,96,3072]{3,2,1,0:T(8,128)(2,1)}, u32[]{:S(2)}) copy-start(bf16[1,2,96,3072]{3,2,1,0:T(8,128)(2,1)} %param.6) | copy-start | bytes 3538948
  8.7 0.9 %copy-start.2 = (f32[64,8,128]{2,1,0:T(8,128)S(1)}, f32[64,8,128]{2,1,0:T(8,128)}, u32[]{:S(2)}) copy-start(f32[64,8,128]{2,1,0:T(8,128)} %param.10) | copy-start | bytes 786436

commit v2 on v1

--- a/solution.py
+++ b/solution.py
@@ -11,21 +11,41 @@
 MESH = pl.DeviceIdType.MESH
 F32 = jnp.float32
 BF16 = jnp.bfloat16
-FAR = ((0, 1), (2, 3))
+SEND_AT = (0, 1, 3, 5)
+
+
+def cos_sin(waves, first, rows, order, period, scale):
+    turns = lax.broadcasted_iota(jnp.int32, (rows, order.shape[1]), 0).astype(F32) * order
+    phase = turns - period * jnp.floor((turns + 0.5) * (1.0 / period))
+    quarter = jnp.floor(phase * (4.0 / period) + 0.5)
+    rest = (phase - quarter * (period / 4.0)) * (2.0 * math.pi / period)
+    q = rest * rest
+    s = rest + rest * q * (-1 / 6 + q * (1 / 120 + q * (-1 / 5040 + q * (1 / 362880))))
+    c = 1.0 + q * (-0.5 + q * (1 / 24 + q * (-1 / 720 + q * (1 / 40320 - q * (1 / 3628800)))))
+    odd = (quarter == 1.0) | (quarter == 3.0)
+    cos = jnp.where(odd, s, c)
+    sin = jnp.where(odd, c, s)
+    cos = jnp.where((quarter == 1.0) | (quarter == 2.0), -cos, cos)
+    sin = jnp.where((quarter == 2.0) | (quarter == 3.0), -sin, sin)
+    waves[0, first : first + rows, :] = cos * scale
+    waves[1, first : first + rows, :] = sin * scale
 
 
 def kernel(
     n_rad,
+    samples_hbm,
+    legendre,
+    order_row,
+    assign,
+    counts,
+    state_hbm,
+    inverses_hbm,
+    out,
     samples,
-    legendre,
-    cos_a,
-    sin_a,
-    cos_b,
-    sin_b,
     state,
+    inverses64,
     inverses,
-    live,
-    out,
+    waves,
     table,
     send_rows,
     got_rows,
@@ -34,12 +54,15 @@
     leg_own,
     leg_got,
     leg_mat,
+    send_first,
+    recv_first,
     send_buf,
     recv_buf,
     acc,
     fields,
     right,
     solved,
+    in_sem,
     own_sem,
     zs_sem,
     zr_sem,
@@ -57,23 +80,20 @@
     n_r = n_rad
     kb = n_r // 4
     comps = 4 * n_r
-    lon_a = cos_a.shape[0]
-    lon_b = cos_b.shape[0]
-    slots = cos_a.shape[1]
+    lon = samples.shape[1]
+    lon_b = 32
+    lon_a = lon // lon_b
+    slots = order_row.shape[1]
 
     barrier = pltpu.get_barrier_semaphore()
-
-    @pl.loop(1, n_rad)
-    def _(i):
-        peer = (rad + i) % n_rad
-        pl.semaphore_signal(barrier, inc=1, device_id=(peer, lat), device_id_type=MESH)
-        pl.semaphore_signal(barrier, inc=1, device_id=(peer, other), device_id_type=MESH)
 
     pl.semaphore_signal(barrier, inc=1, device_id=(rad, other), device_id_type=MESH)
     for d in range(2):
         pl.semaphore_signal(barrier, inc=1, device_id=(rad, y_next[d]), device_id_type=MESH)
 
-    tile_of = [(y // 2 + o) % 4 for o in (2, 1, 3, 0)]
+    odd = y % 2
+    way_a, way_b = 1 - odd, odd
+    tile_of = [(y // 2 + o) % 4 for o in (2, 1 + 2 * odd, 3 + 2 * odd, 0)]
 
     def own_copy(c):
         lanes = pl.multiple_of(z * 512 + tile_of[c] * 128, 128)
@@ -92,37 +112,64 @@
             device_id_type=MESH,
         )
 
+    inputs = [
+        pltpu.make_async_copy(src, dst, in_sem.at[i])
+        for i, (src, dst) in enumerate(
+            ((samples_hbm, samples), (state_hbm, state), (inverses_hbm, inverses64))
+        )
+    ]
+    for copy in inputs:
+        copy.start()
     for c in range(4):
         own_copy(c).start()
 
-    @pl.loop(0, lon_a)
-    def _(a):
-        ca = cos_a[pl.ds(a, 1), :]
-        sa = sin_a[pl.ds(a, 1), :]
-        cb = cos_b[...]
-        sb = sin_b[...]
+    order = order_row[...].astype(F32)
+    cos_sin(waves, 0, lon_a, order, lon_a, 1.0)
+    cos_sin(waves, lon_a, lon_b, order, lon, 1.0 / math.sqrt(lon))
+
+    def table_row(a):
+        ca = waves[0, pl.ds(a, 1), :]
+        sa = waves[1, pl.ds(a, 1), :]
+        cb = waves[0, lon_a : lon_a + lon_b, :]
+        sb = waves[1, lon_a : lon_a + lon_b, :]
         at = pl.multiple_of(a * lon_b, lon_b)
         table[pl.ds(at, lon_b), 0:slots] = (ca * cb - sa * sb).astype(BF16)
         table[pl.ds(at, lon_b), slots : 2 * slots] = (-(sa * cb + ca * sb)).astype(BF16)
 
+    per = lon_a // n_rad
+
+    @pl.loop(0, n_rad)
+    def _(i):
+        @pl.when(i > 0)
+        def _():
+            peer = (rad + i) % n_rad
+            pl.semaphore_signal(barrier, inc=1, device_id=(peer, lat), device_id_type=MESH)
+            pl.semaphore_signal(barrier, inc=1, device_id=(peer, other), device_id_type=MESH)
+
+        for k in range(per):
+            table_row(i * per + k)
+
     pl.semaphore_wait(barrier, 2 * (n_rad - 1) + 3)
-    for c in range(4):
-        z_copy(c).start()
-
+    def z_start(place):
+        for c in range(4):
+            if SEND_AT[c] == place:
+                z_copy(c).start()
+
+    z_start(0)
+    inputs[0].wait()
     fourier = jnp.dot(samples[...], table[...], preferred_element_type=F32)
     fourier = fourier.astype(BF16).astype(F32)
+    wide = []
     for f in range(2):
         part = fourier[96 * f : 96 * (f + 1)]
-        part = jnp.concatenate([part, jnp.zeros((32, 2 * slots), F32)], axis=0)
-        flipped = part.T
-        both = jnp.concatenate(
-            [
-                flipped[:slots].reshape(n_rad, 8, 128),
-                flipped[slots:].reshape(n_rad, 8, 128),
-            ],
-            axis=1,
-        )
-        send_rows[:, 16 * f : 16 * (f + 1), :] = both.astype(BF16)
+        part = jnp.concatenate([part, jnp.zeros((32, 2 * slots), F32)], axis=0).T
+        wide += [part[:slots], part[slots:]]
+    free = lax.broadcasted_iota(jnp.int32, (slots, 128), 1) >= 96
+    packed = [
+        jnp.where(free, pltpu.roll(wide[3], 96 - 32 * c, 1), wide[c]).reshape(n_rad, 8, 128)
+        for c in range(3)
+    ]
+    send_rows[...] = jnp.concatenate(packed, axis=1).astype(BF16)
 
     def a2a(peer, other_side):
         return pltpu.make_async_remote_copy(
@@ -143,6 +190,7 @@
         a2a(peer, 1).start()
 
     got_rows[z, rad] = send_rows[rad]
+    z_start(1)
 
     leg_mat[:, :, :, 96:128, :] = jnp.zeros((2, 8, 4, 32, 128), BF16)
     leg_mat[:, :, :, 224:256, :] = jnp.zeros((2, 8, 4, 32, 128), BF16)
@@ -165,6 +213,9 @@
         own_copy(c).wait()
         lay(leg_own, 0, tile_of[c])
 
+    inputs[1].wait()
+    inputs[2].wait()
+    inverses[...] = jnp.concatenate([inverses64[...], inverses64[...]], axis=1)
     for p in range(4):
         pair = jnp.concatenate(
             [state[pl.ds(2 * p, 64, stride=8), :], state[pl.ds(2 * p + 1, 64, stride=8), :]], axis=0
@@ -173,7 +224,16 @@
 
     spacing = 0.65 / (n_r + 1)
     radius = [0.35 + 0.65 * (i + 1.0) / (n_r + 1) for i in range(n_r)]
-    degree = (lat * 64 + lax.broadcasted_iota(jnp.int32, (1, 128), 1) % 64).astype(F32)
+    lane = lax.broadcasted_iota(jnp.int32, (1, 128), 1)
+    left = lane < 64
+    degree_id = lat * 64 + jnp.where(left, lane, lane - 64)
+    degree = degree_id.astype(F32)
+    live = []
+    for p in range(4):
+        lo, hi = assign[rad * 8 + 2 * p], assign[rad * 8 + 2 * p + 1]
+        start = jnp.where(left, lo, hi)
+        stop = jnp.where(left, lo + counts[lo], hi + counts[hi])
+        live.append((degree_id >= start) & (degree_id < stop))
     square = 0.5 * spacing * spacing * degree * (degree + 1.0)
     for i in range(n_r):
         now = fields[pl.ds(i, 16, stride=n_r), :]
@@ -185,12 +245,17 @@
             value = value + (0.5 - 0.5 * ratio) * fields[pl.ds(i - 1, 16, stride=n_r), :]
         right[pl.ds(i, 16, stride=n_r), :] = value
 
+    lanes = lax.broadcasted_iota(jnp.int32, (n_r, 128), 1)
+
     def regroup(band, side):
-        rows32[...] = got_rows[band].reshape(n_rad * 32, 128).astype(F32)
+        rows32[...] = got_rows[band].astype(F32).reshape(n_rad * 24, 128)
         for s in range(8):
-            for c in range(4):
+            parts = [rows32[pl.ds(8 * c + s, n_r, stride=24), :] for c in range(3)]
+            last = jnp.where(lanes < 32, pltpu.roll(parts[0], 32, 1), pltpu.roll(parts[1], 64, 1))
+            last = jnp.where(lanes < 64, last, pltpu.roll(parts[2], 96, 1))
+            for c, part in enumerate(parts + [last]):
                 modes[side, s // 2, n_r * c : n_r * (c + 1), 128 * (s % 2) : 128 * (s % 2 + 1)] = (
-                    rows32[pl.ds(8 * c + s, n_r, stride=32), :].astype(BF16)
+                    part.astype(BF16)
                 )
 
     def arrival(side, first):
@@ -205,8 +270,10 @@
         )
 
     arrival(0, 1).wait_recv()
+    z_start(2)
     regroup(z, 0)
     arrival(1, 0).wait_recv()
+    z_start(3)
     regroup(1 - z, 1)
 
     def own(d, p):
@@ -217,41 +284,64 @@
             total = band if total is None else total + band
         return total
 
-    def hop(way, h, p):
+    def hop(way, h, p, first):
         i = (way * 4 + h - 1) * 4 + p
         return pltpu.make_async_remote_copy(
-            src_ref=send_buf.at[way, h - 1, p],
-            dst_ref=recv_buf.at[way, h - 1, p],
+            src_ref=send_first.at[way, p] if first else send_buf.at[way, h - 1, p],
+            dst_ref=recv_first.at[way, p] if first else recv_buf.at[way, h - 1, p],
             send_sem=rs_sem.at[i],
             recv_sem=rr_sem.at[i],
-            device_id=(rad, y_next[way]),
+            device_id=(rad, z * 8 + (y + 1 + 6 * way) % 8),
             device_id_type=MESH,
         )
 
-    for h in (4, 3, 2, 1):
-        for c in {4: (0,), 3: (1, 2), 2: (), 1: (3,)}[h]:
-            z_copy(c).wait_recv()
-            lay(leg_got, 1, tile_of[c])
-        for p in range(4):
-            for way in range(2):
-                if h == 4 and p not in FAR[way]:
-                    continue
-                d = (y + h) % 8 if way == 0 else (y + 8 - h) % 8
-                total = own(d, p)
-                if h < 3 or (h == 3 and p in FAR[way]):
-                    hop(way, h + 1, p).wait_recv()
+    def steps(way, h, start):
+        for i in range(2):
+            p = 2 * way + i if start == 4 else 2 * (1 - way) + i
+            total = own((y + h + way * (8 - 2 * h)) % 8, p)
+            if h == start:
+                send_first[way, p] = total.astype(BF16)
+            else:
+                hop(way, h + 1, p, h + 1 == start).wait_recv()
+                if h + 1 == start:
+                    total = total + recv_first[way, p].astype(F32)
+                else:
                     total = total + recv_buf[way, h, p]
                 send_buf[way, h - 1, p] = total
-                hop(way, h, p).start()
+            hop(way, h, p, h == start).start()
+
+    def block(c):
+        z_copy(c).wait_recv()
+        lay(leg_got, 1, tile_of[c])
+        z_start(4 + c)
+
+    block(0)
+    steps(way_a, 4, 4)
+    steps(way_b, 4, 4)
+    steps(way_a, 3, 3)
+    steps(way_a, 3, 4)
+    block(1)
+    steps(way_b, 3, 3)
+    steps(way_b, 3, 4)
+    steps(way_b, 2, 3)
+    steps(way_b, 2, 4)
+    block(2)
+    steps(way_a, 2, 3)
+    steps(way_a, 2, 4)
+    steps(way_a, 1, 3)
+    steps(way_a, 1, 4)
+    block(3)
+    steps(way_b, 1, 3)
+    steps(way_b, 1, 4)
 
     for p in range(4):
         acc[comps * p : comps * (p + 1), :] = own(y, p)
     for p in range(4):
         total = acc[comps * p : comps * (p + 1), :]
         for way in range(2):
-            hop(way, 1, p).wait_recv()
+            hop(way, 1, p, False).wait_recv()
             total = total + recv_buf[way, 0, p]
-        total = jnp.where(live[p : p + 1, :] > 0, total, jnp.zeros_like(total))
+        total = jnp.where(live[p], total, jnp.zeros_like(total))
         rows = slice(comps * p, comps * (p + 1))
         right[rows, :] = right[rows, :] + total
 
@@ -296,62 +386,51 @@
         z_copy(c).wait_send()
     arrival(0, 1).wait_send()
     arrival(1, 0).wait_send()
-    for h in (4, 3, 2, 1):
+    for way in range(2):
         for p in range(4):
-            for way in range(2):
-                if h < 4 or p in FAR[way]:
-                    hop(way, h, p).wait_send()
+            start = 4 if p // 2 == way else 3
+            for h in range(1, start + 1):
+                hop(way, h, p, h == start).wait_send()
 
 
 def body(n_rad, samples, legendre, assign, counts, spectral_state, inverses):
     lon = samples.shape[3]
-    lon_b = 32
-    lon_a = lon // lon_b
-    rad = lax.axis_index("rad")
-    lat = lax.axis_index("lat")
     kb = inverses.shape[2]
-    n_r = 4 * kb
-    comps = 4 * n_r
-    order = assign[None, :]
-    phase_a = jnp.arange(lon_a, dtype=jnp.int32)[:, None] * order % lon_a
-    phase_b = jnp.arange(lon_b, dtype=jnp.int32)[:, None] * order % lon
-    angle_a = phase_a.astype(F32) * (2.0 * math.pi / lon_a)
-    angle_b = phase_b.astype(F32) * (2.0 * math.pi / lon)
-    unit = 1.0 / math.sqrt(lon)
-    cos_a, sin_a = jnp.cos(angle_a), jnp.sin(angle_a)
-    cos_b, sin_b = jnp.cos(angle_b) * unit, jnp.sin(angle_b) * unit
-
-    mine = lax.dynamic_slice_in_dim(assign, rad * 8, 8, 0)
-    ids = jnp.arange(counts.shape[0], dtype=jnp.int32)
-    held = jnp.sum(jnp.where(mine[:, None] == ids[None, :], counts[None, :], 0), axis=1)
-    degrees = lat * 64 + jnp.arange(64, dtype=jnp.int32)
-    live = (degrees[None, :] >= mine[:, None]) & (degrees[None, :] < (mine + held)[:, None])
-    live = live.astype(F32).reshape(4, 128)
-
+    comps = 16 * kb
+    slots = assign.shape[0]
     inv = jnp.transpose(inverses, (1, 2, 3, 0)).reshape(4 * kb * kb, 64)
-    inv = jnp.concatenate([inv, inv], axis=1)
 
     vmem = pl.BlockSpec(memory_space=pltpu.VMEM)
+    smem = pl.BlockSpec(memory_space=pltpu.SMEM)
+    hbm = pl.BlockSpec(memory_space=pltpu.HBM)
     out = pl.pallas_call(
         functools.partial(kernel, n_rad),
         out_shape=jax.ShapeDtypeStruct((512, comps), F32),
-        in_specs=[vmem, pl.BlockSpec(memory_space=pl.ANY)] + [vmem] * 7,
+        in_specs=[hbm, hbm, vmem, smem, smem, hbm, hbm],
         out_specs=vmem,
         scratch_shapes=[
-            pltpu.VMEM((lon, 2 * assign.shape[0]), BF16),
-            pltpu.VMEM((n_rad, 32, 128), BF16),
-            pltpu.VMEM((2, n_rad, 32, 128), BF16),
-            pltpu.VMEM((n_rad * 32, 128), F32),
+            pltpu.VMEM((192, lon), BF16),
+            pltpu.VMEM((512, comps), F32),
+            pltpu.VMEM((4 * kb * kb, 64), F32),
+            pltpu.VMEM((4 * kb * kb, 128), F32),
+            pltpu.VMEM((2, lon // 32 + 32, slots), F32),
+            pltpu.VMEM((lon, 2 * slots), BF16),
+            pltpu.VMEM((n_rad, 24, 128), BF16),
+            pltpu.VMEM((2, n_rad, 24, 128), BF16),
+            pltpu.VMEM((n_rad * 24, 128), F32),
             pltpu.VMEM((2, 4, comps, 256), BF16),
             pltpu.VMEM((4, 8, 96, 128), BF16),
             pltpu.VMEM((4, 8, 96, 128), BF16),
             pltpu.VMEM((2, 8, 4, 256, 128), BF16),
-            pltpu.VMEM((2, 4, 4, comps, 128), F32),
-            pltpu.VMEM((2, 4, 4, comps, 128), F32),
+            pltpu.VMEM((2, 4, comps, 128), BF16),
+            pltpu.VMEM((2, 4, comps, 128), BF16),
+            pltpu.VMEM((2, 3, 4, comps, 128), F32),
+            pltpu.VMEM((2, 3, 4, comps, 128), F32),
             pltpu.VMEM((4 * comps, 128), F32),
             pltpu.VMEM((4 * comps, 128), F32),
             pltpu.VMEM((4 * comps, 128), F32),
             pltpu.VMEM((4 * comps, 128), F32),
+            pltpu.SemaphoreType.DMA((3,)),
             pltpu.SemaphoreType.DMA((4,)),
             pltpu.SemaphoreType.DMA((4,)),
             pltpu.SemaphoreType.DMA((4,)),
@@ -361,18 +440,16 @@
             pltpu.SemaphoreType.DMA((32,)),
         ],
         compiler_params=pltpu.CompilerParams(
-            collective_id=0, has_side_effects=True, vmem_limit_bytes=48 * 1024 * 1024
+            collective_id=0, has_side_effects=True, vmem_limit_bytes=60 * 1024 * 1024
         ),
     )(
         samples.reshape(192, lon),
         legendre,
-        cos_a,
-        sin_a,
-        cos_b,
-        sin_b,
+        assign.reshape(1, slots),
+        assign,
+        counts,
         spectral_state.reshape(512, comps),
         inv,
-        live,
     )
     return out.reshape(64, 8, comps)
 

time: 82.2 us -> 58.8 us (0.72)
  Pallas kernels: 71.6 us -> 57 us
  other arithmetic: 4.65 us -> 0 us
  local copies, waits for them, and re-layouts: 5.64 us -> 1.67 us
    pallas_call x1, Pallas kernels: 71.6 us -> 57 us  [body(): pl.pallas_call(functools.partial(kernel, n_rad), out_shape=jax.ShapeDtype...]
    unnamed x7 -> x1, local copies, waits for them, and re-layouts: 4.33 us -> 1.67 us
    sin x1 -> x0, other arithmetic: 1.1 us -> none  [body(): cos_a, sin_a = (jnp.cos(angle_a), jnp.sin(angle_a))]
    concatenate x1 -> x0, other arithmetic: 1.08 us -> none  [body(): inv = jnp.concatenate([inv, inv], axis=1)]
    reduce_sum x1 -> x0, other arithmetic: 0.86 us -> none  [body(): jnp.sum(jnp.where(mine[:, None] == ids[None, :], counts[None, :], 0), axi...]
    mul x1 -> x0, other arithmetic: 0.84 us -> none  [body(): cos_b, sin_b = (jnp.cos(angle_b) * unit, jnp.sin(angle_b) * unit)]
where the time goes in v2:
time: 58.8 us; the launch traced here: 58.6 us
  Pallas kernels  57 us (97%)
  local copies, waits for them, and re-layouts  1.67 us (3%)
    pallas_call x1, Pallas kernels, body(): pl.pallas_call(functools.partial(kernel, n_rad), out_shape=jax.ShapeDtype...  57 us
    unnamed x1, local copies, waits for them, and re-layouts  1.67 us

profile of v2, /device:TPU:6, one launch (start us, length us, event | category | flops | bytes accessed | tf_op | source)
XLA Modules:
  0.0 58.6 jit_solution(17164011754197365136)
XLA Ops:
  0.0 57.0 %shard_map.64 = f32[512,128]{1,0:T(8,128)} custom-call(bf16[192,3072]{1,0:T(8,128)(2,1)} %bitcast.7, bf16[8,96,1024]{2,1,0:T(8,128)(2,1)} %legendre.1, s32[1,256]{1,0:T(1,128)} %bitcast.11, s32[256]{0:T(256)} %assign.1, s32[256]{0:T(256)} %counts.1, f32[512,128]{1,0:T(8,128)} %bitcast.9, f32[256,64]{1,0:T(8,128)} %bitcast.10), custom_call_target="tpu_custom_call" | custom-call | tf_op jit(solution)/shard_map/pallas_call | solution.py:406
  57.0 1.7 %copy.8 = f32[64,8,128]{2,1,0:T(8,128)} copy(f32[64,8,128]{2,1,0:T(8,128)} %bitcast.8) | data formatting | bytes 524288

commit v3 on v2

--- a/solution.py
+++ b/solution.py
@@ -12,6 +12,8 @@
 F32 = jnp.float32
 BF16 = jnp.bfloat16
 SEND_AT = (0, 1, 3, 5)
+LONG = 1
+WAIT_FIRST = True
 
 
 def cos_sin(waves, first, rows, order, period, scale):
@@ -54,14 +56,15 @@
     leg_own,
     leg_got,
     leg_mat,
-    send_first,
-    recv_first,
+    send_half,
+    recv_half,
     send_buf,
     recv_buf,
     acc,
     fields,
     right,
     solved,
+    column_sem,
     in_sem,
     own_sem,
     zs_sem,
@@ -87,9 +90,22 @@
 
     barrier = pltpu.get_barrier_semaphore()
 
+    n_zh = n_rad // 8
+    zh, xc = rad // 8, rad % 8
+
+    def row_signal(semaphore):
+        for i in range(1, 8):
+            peer = zh * 8 + (xc + i) % 8
+            pl.semaphore_signal(semaphore, inc=1, device_id=(peer, lat), device_id_type=MESH)
+
     pl.semaphore_signal(barrier, inc=1, device_id=(rad, other), device_id_type=MESH)
     for d in range(2):
         pl.semaphore_signal(barrier, inc=1, device_id=(rad, y_next[d]), device_id_type=MESH)
+    for i in range(1, n_zh):
+        peer = (zh + i) % n_zh * 8 + xc
+        pl.semaphore_signal(barrier, inc=1, device_id=(peer, lat), device_id_type=MESH)
+        pl.semaphore_signal(barrier, inc=1, device_id=(peer, other), device_id_type=MESH)
+    row_signal(barrier)
 
     odd = y % 2
     way_a, way_b = 1 - odd, odd
@@ -136,26 +152,28 @@
         table[pl.ds(at, lon_b), 0:slots] = (ca * cb - sa * sb).astype(BF16)
         table[pl.ds(at, lon_b), slots : 2 * slots] = (-(sa * cb + ca * sb)).astype(BF16)
 
-    per = lon_a // n_rad
-
-    @pl.loop(0, n_rad)
-    def _(i):
-        @pl.when(i > 0)
-        def _():
-            peer = (rad + i) % n_rad
-            pl.semaphore_signal(barrier, inc=1, device_id=(peer, lat), device_id_type=MESH)
-            pl.semaphore_signal(barrier, inc=1, device_id=(peer, other), device_id_type=MESH)
-
-        for k in range(per):
-            table_row(i * per + k)
-
-    pl.semaphore_wait(barrier, 2 * (n_rad - 1) + 3)
     def z_start(place):
         for c in range(4):
             if SEND_AT[c] == place:
                 z_copy(c).start()
 
-    z_start(0)
+    def greet():
+        pl.semaphore_wait(barrier, 7 + 2 * n_zh - 1 + 2)
+        z_start(0)
+        row_signal(column_sem)
+
+    if WAIT_FIRST:
+        greet()
+    per = 4
+
+    @pl.loop(0, lon_a // per)
+    def _(i):
+        for k in range(per):
+            table_row(i * per + k)
+
+    if not WAIT_FIRST:
+        greet()
+
     inputs[0].wait()
     fourier = jnp.dot(samples[...], table[...], preferred_element_type=F32)
     fourier = fourier.astype(BF16).astype(F32)
@@ -181,6 +199,7 @@
             device_id_type=MESH,
         )
 
+    pl.semaphore_wait(column_sem, 7)
     a2a(rad, 1).start()
 
     @pl.loop(1, n_rad)
@@ -284,11 +303,11 @@
             total = band if total is None else total + band
         return total
 
-    def hop(way, h, p, first):
+    def hop(way, h, p):
         i = (way * 4 + h - 1) * 4 + p
         return pltpu.make_async_remote_copy(
-            src_ref=send_first.at[way, p] if first else send_buf.at[way, h - 1, p],
-            dst_ref=recv_first.at[way, p] if first else recv_buf.at[way, h - 1, p],
+            src_ref=send_half.at[way, h - 1 - LONG, p] if h > LONG else send_buf.at[way, h - 1, p],
+            dst_ref=recv_half.at[way, h - 1 - LONG, p] if h > LONG else recv_buf.at[way, h - 1, p],
             send_sem=rs_sem.at[i],
             recv_sem=rr_sem.at[i],
             device_id=(rad, z * 8 + (y + 1 + 6 * way) % 8),
@@ -299,16 +318,17 @@
         for i in range(2):
             p = 2 * way + i if start == 4 else 2 * (1 - way) + i
             total = own((y + h + way * (8 - 2 * h)) % 8, p)
-            if h == start:
-                send_first[way, p] = total.astype(BF16)
-            else:
-                hop(way, h + 1, p, h + 1 == start).wait_recv()
-                if h + 1 == start:
-                    total = total + recv_first[way, p].astype(F32)
+            if h < start:
+                hop(way, h + 1, p).wait_recv()
+                if h + 1 > LONG:
+                    total = total + recv_half[way, h - LONG, p].astype(F32)
                 else:
                     total = total + recv_buf[way, h, p]
+            if h > LONG:
+                send_half[way, h - 1 - LONG, p] = total.astype(BF16)
+            else:
                 send_buf[way, h - 1, p] = total
-            hop(way, h, p, h == start).start()
+            hop(way, h, p).start()
 
     def block(c):
         z_copy(c).wait_recv()
@@ -339,7 +359,7 @@
     for p in range(4):
         total = acc[comps * p : comps * (p + 1), :]
         for way in range(2):
-            hop(way, 1, p, False).wait_recv()
+            hop(way, 1, p).wait_recv()
             total = total + recv_buf[way, 0, p]
         total = jnp.where(live[p], total, jnp.zeros_like(total))
         rows = slice(comps * p, comps * (p + 1))
@@ -390,7 +410,7 @@
         for p in range(4):
             start = 4 if p // 2 == way else 3
             for h in range(1, start + 1):
-                hop(way, h, p, h == start).wait_send()
+                hop(way, h, p).wait_send()
 
 
 def body(n_rad, samples, legendre, assign, counts, spectral_state, inverses):
@@ -422,14 +442,15 @@
             pltpu.VMEM((4, 8, 96, 128), BF16),
             pltpu.VMEM((4, 8, 96, 128), BF16),
             pltpu.VMEM((2, 8, 4, 256, 128), BF16),
-            pltpu.VMEM((2, 4, comps, 128), BF16),
-            pltpu.VMEM((2, 4, comps, 128), BF16),
-            pltpu.VMEM((2, 3, 4, comps, 128), F32),
-            pltpu.VMEM((2, 3, 4, comps, 128), F32),
+            pltpu.VMEM((2, 4 - LONG, 4, comps, 128), BF16),
+            pltpu.VMEM((2, 4 - LONG, 4, comps, 128), BF16),
+            pltpu.VMEM((2, LONG, 4, comps, 128), F32),
+            pltpu.VMEM((2, LONG, 4, comps, 128), F32),
             pltpu.VMEM((4 * comps, 128), F32),
             pltpu.VMEM((4 * comps, 128), F32),
             pltpu.VMEM((4 * comps, 128), F32),
             pltpu.VMEM((4 * comps, 128), F32),
+            pltpu.SemaphoreType.REGULAR,
             pltpu.SemaphoreType.DMA((3,)),
             pltpu.SemaphoreType.DMA((4,)),
             pltpu.SemaphoreType.DMA((4,)),

time: 58.8 us -> 52.8 us (0.90)
  Pallas kernels: 57 us -> 51 us
    pallas_call x1, Pallas kernels: 57 us -> 51 us  [body(): pl.pallas_call(functools.partial(kernel, n_rad), out_shape=jax.ShapeDtype...]
where the time goes in v3:
time: 52.8 us; the launch traced here: 52.6 us
  Pallas kernels  51 us (97%)
  local copies, waits for them, and re-layouts  1.67 us (3%)
    pallas_call x1, Pallas kernels, body(): pl.pallas_call(functools.partial(kernel, n_rad), out_shape=jax.ShapeDtype...  51 us
    unnamed x1, local copies, waits for them, and re-layouts  1.67 us

profile of v3, /device:TPU:6, one launch (start us, length us, event | category | flops | bytes accessed | tf_op | source)
XLA Modules:
  0.0 52.6 jit_solution(18102170042945754455)
XLA Ops:
  0.0 51.0 %shard_map.64 = f32[512,128]{1,0:T(8,128)} custom-call(bf16[192,3072]{1,0:T(8,128)(2,1)} %bitcast.7, bf16[8,96,1024]{2,1,0:T(8,128)(2,1)} %legendre.1, s32[1,256]{1,0:T(1,128)} %bitcast.11, s32[256]{0:T(256)} %assign.1, s32[256]{0:T(256)} %counts.1, f32[512,128]{1,0:T(8,128)} %bitcast.9, f32[256,64]{1,0:T(8,128)} %bitcast.10), custom_call_target="tpu_custom_call" | custom-call | tf_op jit(solution)/shard_map/pallas_call | solution.py:426
  51.0 1.7 %copy.8 = f32[64,8,128]{2,1,0:T(8,128)} copy(f32[64,8,128]{2,1,0:T(8,128)} %bitcast.8) | data formatting | bytes 524288

commit v4 on v3

--- a/solution.py
+++ b/solution.py
@@ -12,7 +12,6 @@
 F32 = jnp.float32
 BF16 = jnp.bfloat16
 SEND_AT = (0, 1, 3, 5)
-LONG = 1
 WAIT_FIRST = True
 
 
@@ -56,11 +55,9 @@
     leg_own,
     leg_got,
     leg_mat,
-    send_half,
-    recv_half,
     send_buf,
     recv_buf,
-    acc,
+    mine,
     fields,
     right,
     solved,
@@ -200,19 +197,23 @@
         )
 
     pl.semaphore_wait(column_sem, 7)
-    a2a(rad, 1).start()
 
     @pl.loop(1, n_rad)
     def _(i):
-        peer = (rad + i) % n_rad
-        a2a(peer, 0).start()
-        a2a(peer, 1).start()
+        a2a((rad + i) % n_rad, 0).start()
+
+    a2a(rad, 1).start()
+
+    @pl.loop(1, n_rad)
+    def _(i):
+        a2a((rad + i) % n_rad, 1).start()
+
 
     got_rows[z, rad] = send_rows[rad]
     z_start(1)
 
-    leg_mat[:, :, :, 96:128, :] = jnp.zeros((2, 8, 4, 32, 128), BF16)
-    leg_mat[:, :, :, 224:256, :] = jnp.zeros((2, 8, 4, 32, 128), BF16)
+    leg_mat[:, :, :, 96:128, :] = jnp.zeros((2, 4, 4, 32, 256), BF16)
+    leg_mat[:, :, :, 224:256, :] = jnp.zeros((2, 4, 4, 32, 256), BF16)
     low = lax.broadcasted_iota(jnp.int32, (96, 128), 1) < 64
 
     def lay(source, band, tile):
@@ -223,10 +224,10 @@
             ra = pltpu.roll(a, 64, 1)
             rb = pltpu.roll(b, 64, 1)
             zero = jnp.zeros_like(a)
-            leg_mat[band, 2 * tile, p, 0:96, :] = jnp.where(low, a, zero).astype(BF16)
-            leg_mat[band, 2 * tile, p, 128:224, :] = jnp.where(low, zero, rb).astype(BF16)
-            leg_mat[band, 2 * tile + 1, p, 0:96, :] = jnp.where(low, ra, zero).astype(BF16)
-            leg_mat[band, 2 * tile + 1, p, 128:224, :] = jnp.where(low, zero, b).astype(BF16)
+            leg_mat[band, tile, p, 0:96, 0:128] = jnp.where(low, a, zero).astype(BF16)
+            leg_mat[band, tile, p, 128:224, 0:128] = jnp.where(low, zero, rb).astype(BF16)
+            leg_mat[band, tile, p, 0:96, 128:256] = jnp.where(low, ra, zero).astype(BF16)
+            leg_mat[band, tile, p, 128:224, 128:256] = jnp.where(low, zero, b).astype(BF16)
 
     for c in range(4):
         own_copy(c).wait()
@@ -288,26 +289,35 @@
             device_id_type=MESH,
         )
 
+    def share(side, tile):
+        for p in range(4):
+            band = jnp.dot(modes[side, p], leg_mat[side, tile, p], preferred_element_type=F32)
+            band = band.astype(BF16).astype(F32)
+            for k in range(2):
+                part = band[:, 128 * k : 128 * (k + 1)]
+                mine[2 * tile + k, p] = part if side == 0 else mine[2 * tile + k, p] + part
+
+    def block(c):
+        z_copy(c).wait_recv()
+        lay(leg_got, 1, tile_of[c])
+        z_start(4 + c)
+
     arrival(0, 1).wait_recv()
     z_start(2)
     regroup(z, 0)
+    for c in range(4):
+        share(0, tile_of[c])
+    block(0)
     arrival(1, 0).wait_recv()
     z_start(3)
     regroup(1 - z, 1)
-
-    def own(d, p):
-        total = None
-        for side in range(2):
-            band = jnp.dot(modes[side, p], leg_mat[side, d, p], preferred_element_type=F32)
-            band = band.astype(BF16).astype(F32)
-            total = band if total is None else total + band
-        return total
+    share(1, tile_of[0])
 
     def hop(way, h, p):
         i = (way * 4 + h - 1) * 4 + p
         return pltpu.make_async_remote_copy(
-            src_ref=send_half.at[way, h - 1 - LONG, p] if h > LONG else send_buf.at[way, h - 1, p],
-            dst_ref=recv_half.at[way, h - 1 - LONG, p] if h > LONG else recv_buf.at[way, h - 1, p],
+            src_ref=send_buf.at[way, h - 1, p],
+            dst_ref=recv_buf.at[way, h - 1, p],
             send_sem=rs_sem.at[i],
             recv_sem=rr_sem.at[i],
             device_id=(rad, z * 8 + (y + 1 + 6 * way) % 8),
@@ -317,50 +327,39 @@
     def steps(way, h, start):
         for i in range(2):
             p = 2 * way + i if start == 4 else 2 * (1 - way) + i
-            total = own((y + h + way * (8 - 2 * h)) % 8, p)
+            total = mine[(y + h + way * (8 - 2 * h)) % 8, p]
             if h < start:
                 hop(way, h + 1, p).wait_recv()
-                if h + 1 > LONG:
-                    total = total + recv_half[way, h - LONG, p].astype(F32)
-                else:
-                    total = total + recv_buf[way, h, p]
-            if h > LONG:
-                send_half[way, h - 1 - LONG, p] = total.astype(BF16)
-            else:
-                send_buf[way, h - 1, p] = total
+                total = total + recv_buf[way, h, p].astype(F32)
+            send_buf[way, h - 1, p] = total.astype(BF16)
             hop(way, h, p).start()
 
-    def block(c):
-        z_copy(c).wait_recv()
-        lay(leg_got, 1, tile_of[c])
-        z_start(4 + c)
-
-    block(0)
     steps(way_a, 4, 4)
     steps(way_b, 4, 4)
     steps(way_a, 3, 3)
     steps(way_a, 3, 4)
     block(1)
+    share(1, tile_of[1])
     steps(way_b, 3, 3)
     steps(way_b, 3, 4)
     steps(way_b, 2, 3)
     steps(way_b, 2, 4)
     block(2)
+    share(1, tile_of[2])
     steps(way_a, 2, 3)
     steps(way_a, 2, 4)
     steps(way_a, 1, 3)
     steps(way_a, 1, 4)
     block(3)
+    share(1, tile_of[3])
     steps(way_b, 1, 3)
     steps(way_b, 1, 4)
 
     for p in range(4):
-        acc[comps * p : comps * (p + 1), :] = own(y, p)
-    for p in range(4):
-        total = acc[comps * p : comps * (p + 1), :]
+        total = mine[y, p]
         for way in range(2):
             hop(way, 1, p).wait_recv()
-            total = total + recv_buf[way, 0, p]
+            total = total + recv_buf[way, 0, p].astype(F32)
         total = jnp.where(live[p], total, jnp.zeros_like(total))
         rows = slice(comps * p, comps * (p + 1))
         right[rows, :] = right[rows, :] + total
@@ -441,12 +440,10 @@
             pltpu.VMEM((2, 4, comps, 256), BF16),
             pltpu.VMEM((4, 8, 96, 128), BF16),
             pltpu.VMEM((4, 8, 96, 128), BF16),
-            pltpu.VMEM((2, 8, 4, 256, 128), BF16),
-            pltpu.VMEM((2, 4 - LONG, 4, comps, 128), BF16),
-            pltpu.VMEM((2, 4 - LONG, 4, comps, 128), BF16),
-            pltpu.VMEM((2, LONG, 4, comps, 128), F32),
-            pltpu.VMEM((2, LONG, 4, comps, 128), F32),
-            pltpu.VMEM((4 * comps, 128), F32),
+            pltpu.VMEM((2, 4, 4, 256, 256), BF16),
+            pltpu.VMEM((2, 4, 4, comps, 128), BF16),
+            pltpu.VMEM((2, 4, 4, comps, 128), BF16),
+            pltpu.VMEM((8, 4, comps, 128), F32),
             pltpu.VMEM((4 * comps, 128), F32),
             pltpu.VMEM((4 * comps, 128), F32),
             pltpu.VMEM((4 * comps, 128), F32),

time: 52.8 us -> 51 us (0.966)
  the two profiles are of different devices: /device:TPU:6 before, /device:TPU:16 now
where the time goes in v4:
time: 51 us; the launch traced here: 50.8 us
  Pallas kernels  49.2 us (96%)
  local copies, waits for them, and re-layouts  1.67 us (3%)
    pallas_call x1, Pallas kernels, body(): pl.pallas_call(functools.partial(kernel, n_rad), out_shape=jax.ShapeDtype...  49.2 us
    unnamed x1, local copies, waits for them, and re-layouts  1.67 us

profile of v4, /device:TPU:16, one launch (start us, length us, event | category | flops | bytes accessed | tf_op | source)
XLA Modules:
  0.0 50.8 jit_solution(6497394715443267349)
XLA Ops:
  0.0 49.2 %shard_map.64 = f32[512,128]{1,0:T(8,128)} custom-call(bf16[192,3072]{1,0:T(8,128)(2,1)} %bitcast.7, bf16[8,96,1024]{2,1,0:T(8,128)(2,1)} %legendre.1, s32[1,256]{1,0:T(1,128)} %bitcast.11, s32[256]{0:T(256)} %assign.1, s32[256]{0:T(256)} %counts.1, f32[512,128]{1,0:T(8,128)} %bitcast.9, f32[256,64]{1,0:T(8,128)} %bitcast.10), custom_call_target="tpu_custom_call" | custom-call | tf_op jit(solution)/shard_map/pallas_call | solution.py:425
  49.2 1.7 %copy.8 = f32[64,8,128]{2,1,0:T(8,128)} copy(f32[64,8,128]{2,1,0:T(8,128)} %bitcast.8) | data formatting | bytes 524288

commit v5 on v4

--- a/solution.py
+++ b/solution.py
@@ -200,13 +200,13 @@
 
     @pl.loop(1, n_rad)
     def _(i):
-        a2a((rad + i) % n_rad, 0).start()
+        a2a((rad + (i + 14) % 31 + 1) % n_rad, 0).start()
 
     a2a(rad, 1).start()
 
     @pl.loop(1, n_rad)
     def _(i):
-        a2a((rad + i) % n_rad, 1).start()
+        a2a((rad + (i + 14) % 31 + 1) % n_rad, 1).start()
 
 
     got_rows[z, rad] = send_rows[rad]

time: 51 us -> 50.6 us (level)
  no operation moved by 1% of the time
where the time goes in v5:
time: 50.6 us; the launch traced here: 50.4 us
  Pallas kernels  48.8 us (96%)
  local copies, waits for them, and re-layouts  1.67 us (3%)
    pallas_call x1, Pallas kernels, body(): pl.pallas_call(functools.partial(kernel, n_rad), out_shape=jax.ShapeDtype...  48.8 us
    unnamed x1, local copies, waits for them, and re-layouts  1.67 us

profile of v5, /device:TPU:16, one launch (start us, length us, event | category | flops | bytes accessed | tf_op | source)
XLA Modules:
  0.0 50.4 jit_solution(12368155084627321684)
XLA Ops:
  0.0 48.8 %shard_map.64 = f32[512,128]{1,0:T(8,128)} custom-call(bf16[192,3072]{1,0:T(8,128)(2,1)} %bitcast.7, bf16[8,96,1024]{2,1,0:T(8,128)(2,1)} %legendre.1, s32[1,256]{1,0:T(1,128)} %bitcast.11, s32[256]{0:T(256)} %assign.1, s32[256]{0:T(256)} %counts.1, f32[512,128]{1,0:T(8,128)} %bitcast.9, f32[256,64]{1,0:T(8,128)} %bitcast.10), custom_call_target="tpu_custom_call" | custom-call | tf_op jit(solution)/shard_map/pallas_call | solution.py:425
  48.8 1.7 %copy.8 = f32[64,8,128]{2,1,0:T(8,128)} copy(f32[64,8,128]{2,1,0:T(8,128)} %bitcast.8) | data formatting | bytes 524288

commit v6 on v5

--- a/solution.py
+++ b/solution.py
@@ -11,7 +11,7 @@
 MESH = pl.DeviceIdType.MESH
 F32 = jnp.float32
 BF16 = jnp.bfloat16
-SEND_AT = (0, 1, 3, 5)
+SEND_AT = (0, 1, 3, 5, 5)
 WAIT_FIRST = True
 
 
@@ -115,10 +115,12 @@
         )
 
     def z_copy(c):
-        lanes = pl.multiple_of((1 - z) * 512 + tile_of[c] * 128, 128)
+        tile = tile_of[min(c, 3)]
+        held = pl.ds(0, 8) if c < 3 else pl.ds(4 * (c - 3), 4)
+        lanes = pl.multiple_of((1 - z) * 512 + tile * 128, 128)
         return pltpu.make_async_remote_copy(
-            src_ref=legendre.at[:, :, pl.ds(lanes, 128)],
-            dst_ref=leg_got.at[tile_of[c]],
+            src_ref=legendre.at[held, :, pl.ds(lanes, 128)],
+            dst_ref=leg_got.at[tile, held],
             send_sem=zs_sem.at[c],
             recv_sem=zr_sem.at[c],
             device_id=(rad, other),
@@ -150,7 +152,7 @@
         table[pl.ds(at, lon_b), slots : 2 * slots] = (-(sa * cb + ca * sb)).astype(BF16)
 
     def z_start(place):
-        for c in range(4):
+        for c in range(5):
             if SEND_AT[c] == place:
                 z_copy(c).start()
 
@@ -216,8 +218,8 @@
     leg_mat[:, :, :, 224:256, :] = jnp.zeros((2, 4, 4, 32, 256), BF16)
     low = lax.broadcasted_iota(jnp.int32, (96, 128), 1) < 64
 
-    def lay(source, band, tile):
-        @pl.loop(0, 4)
+    def lay(source, band, tile, first=0, end=4):
+        @pl.loop(first, end)
         def _(p):
             a = source[tile, 2 * p].astype(F32)
             b = source[tile, 2 * p + 1].astype(F32)
@@ -289,8 +291,8 @@
             device_id_type=MESH,
         )
 
-    def share(side, tile):
-        for p in range(4):
+    def share(side, tile, first=0, end=4):
+        for p in range(first, end):
             band = jnp.dot(modes[side, p], leg_mat[side, tile, p], preferred_element_type=F32)
             band = band.astype(BF16).astype(F32)
             for k in range(2):
@@ -299,7 +301,8 @@
 
     def block(c):
         z_copy(c).wait_recv()
-        lay(leg_got, 1, tile_of[c])
+        pairs = (0, 4) if c < 3 else (2 * (c - 3), 2 * (c - 3) + 2)
+        lay(leg_got, 1, tile_of[min(c, 3)], *pairs)
         z_start(4 + c)
 
     arrival(0, 1).wait_recv()
@@ -324,15 +327,17 @@
             device_id_type=MESH,
         )
 
+    def step(way, h, start, p):
+        total = mine[(y + h + way * (8 - 2 * h)) % 8, p]
+        if h < start:
+            hop(way, h + 1, p).wait_recv()
+            total = total + recv_buf[way, h, p].astype(F32)
+        send_buf[way, h - 1, p] = total.astype(BF16)
+        hop(way, h, p).start()
+
     def steps(way, h, start):
         for i in range(2):
-            p = 2 * way + i if start == 4 else 2 * (1 - way) + i
-            total = mine[(y + h + way * (8 - 2 * h)) % 8, p]
-            if h < start:
-                hop(way, h + 1, p).wait_recv()
-                total = total + recv_buf[way, h, p].astype(F32)
-            send_buf[way, h - 1, p] = total.astype(BF16)
-            hop(way, h, p).start()
+            step(way, h, start, 2 * way + i if start == 4 else 2 * (1 - way) + i)
 
     steps(way_a, 4, 4)
     steps(way_b, 4, 4)
@@ -350,10 +355,11 @@
     steps(way_a, 2, 4)
     steps(way_a, 1, 3)
     steps(way_a, 1, 4)
-    block(3)
-    share(1, tile_of[3])
-    steps(way_b, 1, 3)
-    steps(way_b, 1, 4)
+    for q in range(2):
+        block(3 + q)
+        share(1, tile_of[3], 2 * q, 2 * q + 2)
+        for i in range(2):
+            step(way_b, 1, 3, 2 * q + i)
 
     for p in range(4):
         total = mine[y, p]
@@ -401,7 +407,7 @@
         out[pl.ds(2 * p, 64, stride=8), :] = flipped[:64]
         out[pl.ds(2 * p + 1, 64, stride=8), :] = flipped[64:]
 
-    for c in range(4):
+    for c in range(5):
         z_copy(c).wait_send()
     arrival(0, 1).wait_send()
     arrival(1, 0).wait_send()
@@ -450,8 +456,8 @@
             pltpu.SemaphoreType.REGULAR,
             pltpu.SemaphoreType.DMA((3,)),
             pltpu.SemaphoreType.DMA((4,)),
-            pltpu.SemaphoreType.DMA((4,)),
-            pltpu.SemaphoreType.DMA((4,)),
+            pltpu.SemaphoreType.DMA((5,)),
+            pltpu.SemaphoreType.DMA((5,)),
             pltpu.SemaphoreType.DMA((2,)),
             pltpu.SemaphoreType.DMA((2,)),
             pltpu.SemaphoreType.DMA((32,)),

time: 50.6 us -> 50.9 us (level)
  the two profiles are of different devices: /device:TPU:16 before, /device:TPU:8 now
where the time goes in v6:
time: 50.9 us; the launch traced here: 50.7 us
  Pallas kernels  49.1 us (96%)
  local copies, waits for them, and re-layouts  1.67 us (3%)
    pallas_call x1, Pallas kernels, body(): pl.pallas_call(functools.partial(kernel, n_rad), out_shape=jax.ShapeDtype...  49.1 us
    unnamed x1, local copies, waits for them, and re-layouts  1.67 us

profile of v6, /device:TPU:8, one launch (start us, length us, event | category | flops | bytes accessed | tf_op | source)
XLA Modules:
  0.0 50.7 jit_solution(9750769370843216044)
XLA Ops:
  0.0 49.1 %shard_map.64 = f32[512,128]{1,0:T(8,128)} custom-call(bf16[192,3072]{1,0:T(8,128)(2,1)} %bitcast.7, bf16[8,96,1024]{2,1,0:T(8,128)(2,1)} %legendre.1, s32[1,256]{1,0:T(1,128)} %bitcast.11, s32[256]{0:T(256)} %assign.1, s32[256]{0:T(256)} %counts.1, f32[512,128]{1,0:T(8,128)} %bitcast.9, f32[256,64]{1,0:T(8,128)} %bitcast.10), custom_call_target="tpu_custom_call" | custom-call | tf_op jit(solution)/shard_map/pallas_call | solution.py:431
  49.1 1.7 %copy.8 = f32[64,8,128]{2,1,0:T(8,128)} copy(f32[64,8,128]{2,1,0:T(8,128)} %bitcast.8) | data formatting | bytes 524288

commit v7 on v6

--- a/solution.py
+++ b/solution.py
@@ -11,7 +11,7 @@
 MESH = pl.DeviceIdType.MESH
 F32 = jnp.float32
 BF16 = jnp.bfloat16
-SEND_AT = (0, 1, 3, 5, 5)
+SEND_AT = (0, 1, 3, 3, 5)
 WAIT_FIRST = True
 
 

time: 50.9 us -> 50.9 us (level)
  no operation moved by 1% of the time
where the time goes in v7:
time: 50.9 us; the launch traced here: 50.7 us
  Pallas kernels  49.1 us (96%)
  local copies, waits for them, and re-layouts  1.67 us (3%)
    pallas_call x1, Pallas kernels, body(): pl.pallas_call(functools.partial(kernel, n_rad), out_shape=jax.ShapeDtype...  49.1 us
    unnamed x1, local copies, waits for them, and re-layouts  1.67 us

profile of v7, /device:TPU:8, one launch (start us, length us, event | category | flops | bytes accessed | tf_op | source)
XLA Modules:
  0.0 50.7 jit_solution(16407190030393328741)
XLA Ops:
  0.0 49.1 %shard_map.64 = f32[512,128]{1,0:T(8,128)} custom-call(bf16[192,3072]{1,0:T(8,128)(2,1)} %bitcast.7, bf16[8,96,1024]{2,1,0:T(8,128)(2,1)} %legendre.1, s32[1,256]{1,0:T(1,128)} %bitcast.11, s32[256]{0:T(256)} %assign.1, s32[256]{0:T(256)} %counts.1, f32[512,128]{1,0:T(8,128)} %bitcast.9, f32[256,64]{1,0:T(8,128)} %bitcast.10), custom_call_target="tpu_custom_call" | custom-call | tf_op jit(solution)/shard_map/pallas_call | solution.py:431
  49.1 1.7 %copy.8 = f32[64,8,128]{2,1,0:T(8,128)} copy(f32[64,8,128]{2,1,0:T(8,128)} %bitcast.8) | data formatting | bytes 524288
